TPU v7x, 32 devices: a whole 2x2x4 slice. The times are simulated.
32 devices in a mesh: fsdp: 8 (over z, x), ctx: 4 (over y, core).
Axes of the slice: x: 2, y: 2, z: 4, core: 2. Of those that a mesh axis runs over, the one named last changes fastest.
Arguments:
- tokens: bfloat16 [8, 512, 4096], P('fsdp', 'ctx'), may hold values from -6 to 6
- norm_gain: float32 [4096], replicated, may hold values from 0.5 to 1.5
- w_in: bfloat16 [4096, 3, 4096], P(None, None, 'fsdp'), may hold values from -0.09375 to 0.09375
- taps: float32 [3, 3, 4096], P(None, None, 'fsdp'), may hold values from -3 to 3
- decay_rate: float32 [16, 4096], P(None, 'fsdp'), may hold values from 0 to 0.0334, as said below
- residues: float32 [16, 4096], P(None, 'fsdp'), may hold values from -0.12 to 0.12
- skip_gain: float32 [4096], P('fsdp'), may hold values from -4 to 4
- w_out: bfloat16 [4096, 4096], P('fsdp'), may hold values from -0.09375 to 0.09375
Outputs:
- mixed: bfloat16 [8, 512, 4096], P('fsdp', 'ctx')
Inputs may be any that keep to these rules, and one draw needn't show every extreme that they name: `decay_rate`: positive decay rates of the poles, at most 1/30.
All inputs are finite; a program needn't handle non-finite values.
Results may differ from a plain program's by a relative error of at most 0.024.
Values may be sent and summed in bfloat16 or wider, within the bound.
A program may use at most 192 MiB of HBM per device.

v0:
```python
import jax
import jax.numpy as jnp
from jax import lax
from jax.sharding import PartitionSpec as P


def from_behind(value, axis, steps):
    count = lax.axis_size(axis)
    first, last = (max(0, -steps), min(count, count - steps))
    return lax.ppermute(value, axis, [(source, source + steps) for source in range(first, last)])


def shards(tokens, norm_gain, w_in, taps, decay_rate, residues, skip_gain, w_out):
    high = lax.Precision.HIGHEST
    values = tokens.astype(jnp.float32)
    inverse_rms = lax.rsqrt(jnp.mean(values * values, axis=-1, keepdims=True) + 1e-06)
    normed = (values * inverse_rms * norm_gain).astype(jnp.bfloat16)
    model_width = w_in.shape[0]
    channels = w_in.shape[2]
    w_flat = w_in.reshape(model_width, 3 * channels)
    features = jnp.einsum(
        "gtd,de->gte",
        lax.all_gather(normed, "fsdp", axis=0, tiled=True),
        w_flat,
        preferred_element_type=jnp.float32,
    ).astype(jnp.bfloat16)
    groups = features.shape[0]
    length = features.shape[1]
    edge_rows = from_behind(features[:, length - 2 :], "ctx", 1)
    extended = jnp.concatenate([edge_rows, features], axis=1).astype(jnp.float32)
    tap_rows = taps.reshape(taps.shape[0], 3 * channels)
    filtered = (
        tap_rows[0] * extended[:, 2:]
        + tap_rows[1] * extended[:, 1:-1]
        + tap_rows[2] * extended[:, :-2]
    )
    query_part = filtered[:, :, :channels]
    product = filtered[:, :, channels : 2 * channels] * filtered[:, :, 2 * channels :]
    offsets = jnp.arange(length, dtype=jnp.float32)
    powers = jnp.exp(-decay_rate[:, None, :] * offsets[None, :, None])
    kernel = jnp.sum(residues[:, None, :] * powers, axis=0)
    positions = jnp.arange(length, dtype=jnp.int32)
    lag_steps = positions[:, None] - positions[None, :]
    toeplitz = jnp.where(
        (lag_steps >= 0)[:, :, None], kernel[jnp.maximum(lag_steps, 0)], jnp.float32(0.0)
    )
    inside = jnp.einsum("tsc,gsc->gtc", toeplitz, product, precision=high)
    end_pow = jnp.exp(-decay_rate[:, None, :] * (length - 1 - offsets)[None, :, None])
    summary = jnp.einsum("nsc,gsc->gnc", end_pow, product, precision=high)
    decay_all = jnp.exp(-decay_rate * length)
    ctx_count = lax.axis_size("ctx")
    incoming = jnp.zeros_like(summary)
    for hop_step in range(ctx_count - 1):
        incoming = from_behind(
            (decay_all * incoming + summary).astype(jnp.bfloat16), "ctx", 1
        ).astype(jnp.float32)
    enter = residues[:, None, :] * jnp.exp(-decay_rate[:, None, :] * (offsets + 1.0)[None, :, None])
    entering = jnp.einsum("ntc,gnc->gtc", enter, incoming, precision=high)
    response = skip_gain * product + inside + entering
    gated = (query_part * response).astype(jnp.bfloat16).reshape(groups * length, channels)
    summed = lax.psum_scatter(
        jnp.dot(gated, w_out, preferred_element_type=jnp.float32).astype(jnp.bfloat16),
        "fsdp",
        scatter_dimension=0,
        tiled=True,
    ).astype(jnp.float32)
    return (values[0] + summed).astype(jnp.bfloat16)[None]


def solution(mesh):
    in_specs = (
        P("fsdp", "ctx", None),
        P(),
        P(None, None, "fsdp"),
        P(None, None, "fsdp"),
        P(None, "fsdp"),
        P(None, "fsdp"),
        P("fsdp"),
        P("fsdp", None),
    )
    out_specs = P("fsdp", "ctx", None)
    return jax.shard_map(shards, mesh=mesh, in_specs=in_specs, out_specs=out_specs, check_vma=False)
```

profile of v0, /device:TPU:0, one launch (start us, length us, event | category | flops | bytes accessed | tf_op | source)
XLA Modules:
  0.0 530.6 jit_solution(6598417835448091242)
XLA Ops:
  8.1 2.5 fusion.17
  10.7 17.1 %copy.49 = bf16[4096,3,512]{0,2,1:T(8,128)(2,1)} copy(bf16[4096,3,512]{2,0,1:T(8,128)(2,1)} %param.10) | data formatting | bytes 25165824 | tf_op args[2]
  28.1 6.7 %multiply_reduce_fusion = f32[128,512]{0,1:T(8,128)} fusion(f32[16,512]{0,1:T(8,128)S(1)} %copy.52, f32[16,512]{0,1:T(8,128)S(1)} %copy.51), kind=kLoop, calls=%fused_computation.18 | loop fusion | flops 3080192 | bytes 327680 | tf_op jit(solution)/shard_map/reduce_sum | solution.py:41
  34.8 103.6 %all-gather.2.cloned.1.call-done = bf16[8,128,4096]{2,1,0:T(8,128)(2,1)} async-done(((bf16[1,128,4096]{2,1,0:T(8,128)(2,1)}), bf16[8,128,4096]{2,1,0:T(8,128)(2,1)}) %all-gather.2.cloned.1.call-update) | async-done | bytes 8388624 | tf_op jit(solution)/shard_map/all_gather | solution.py:23
  138.4 18.3 %convolution_convert_fusion.1 = bf16[8,128,1536]{2,1,0:T(8,128)(2,1)S(1)} fusion(bf16[8,128,4096]{2,1,0:T(8,128)(2,1)} %all-gather.2.cloned.1.call-done, bf16[4096,1536,1]{0,1,2:T(8,128)(2,1)} %bitcast.44), kind=kOutput, calls=%fused_computation.19 | convolution fusion | flops 12886474752 | bytes 24117248 | tf_op jit(solution)/shard_map/gtd,de->gte/dot_general | solution.py:21
  160.8 1.9 fusion.4
  162.7 2.7 copy-done
  165.3 1.8 slice_multiply_fusion.3
  167.1 2.1 copy.55
  169.3 8.1 %fusion.10 = f32[512,8,16]{2,1,0:T(8,128)} fusion(f32[8,128,512]{1,0,2:T(8,128)S(1)} %copy.55, f32[128]{0:T(128)S(1)} %copy-done.8, f32[16,512]{0,1:T(8,128)S(1)} %copy.52), kind=kOutput, calls=%fused_computation.15 | convolution fusion | flops 101711872 | bytes 2392576 | tf_op jit(solution)/shard_map/nsc,gsc->gnc/dot_general | solution.py:49
  177.3 2.2 copy.58
  179.5 4.5 collective-permute-start.1
  185.7 5.1 collective-permute-start.2
  190.9 64.2 %gather_fusion = f32[16384,512]{1,0:T(8,128)} fusion(f32[128,512]{1,0:T(8,128)S(1)} %copy.53, s32[16384]{0:T(1024)S(1)} %bitcast_clamp_fusion), kind=kCustom, calls=%fused_computation | custom fusion | bytes 67174400 | tf_op jit(solution)/shard_map/gather | solution.py:45
  255.1 35.6 %copy.54 = f32[128,128,512]{1,0,2:T(8,128)} copy(f32[128,128,512]{2,1,0:T(8,128)} %bitcast.43) | data formatting | bytes 67108864 | tf_op jit(solution)/shard_map/gather | solution.py:45
  290.8 4.6 collective-permute-start.3
  295.4 56.5 %fusion = f32[512,8,128]{2,1,0:T(8,128)} fusion(f32[8,128,512]{1,0,2:T(8,128)S(1)} %copy.55, f32[128,128,512]{1,0,2:T(8,128)} %copy.54, pred[128,128]{1,0:T(8,128)(4,1)S(1)} %subtract_compare_fusion), kind=kOutput, calls=%fused_computation.1 | convolution fusion | flops 813694976 | bytes 37765120 | tf_op jit(solution)/shard_map/tsc,gsc->gtc/dot_general | solution.py:47
  351.9 1.9 copy.56
  354.6 5.7 %fusion.6 = f32[512,8,128]{2,1,0:T(8,128)} fusion(bf16[8,16,512]{1,0,2:T(8,128)(2,1)S(1)} %copy.59, f32[128]{0:T(128)S(1)} %iota_add_fusion, f32[16,512]{0,1:T(8,128)S(1)} %copy.52, f32[16,512]{0,1:T(8,128)} %copy-done.2), kind=kOutput, calls=%fused_computation.11 | convolution fusion | flops 102760448 | bytes 2294272 | tf_op jit(solution)/shard_map/ntc,gnc->gtc/dot_general | solution.py:58
  360.3 2.9 copy.60
  363.3 4.9 fusion.18
  368.2 6.7 %convolution_convert_fusion = bf16[1024,4096]{1,0:T(8,128)(2,1)} fusion(bf16[1024,512]{1,0:T(8,128)(2,1)S(1)} %bitcast.45, bf16[512,4096]{1,0:T(8,128)(2,1)S(1)} %copy-done.9), kind=kOutput, calls=%fused_computation.5 | convolution fusion | flops 4299161600 | bytes 13631488 | tf_op jit(solution)/shard_map/dot_general | solution.py:62
  374.9 146.4 %reduce-scatter.2.cloned.1.call-done = bf16[128,4096]{1,0:T(8,128)(2,1)} async-done(((bf16[1024,4096]{1,0:T(8,128)(2,1)}), bf16[128,4096]{1,0:T(8,128)(2,1)}) %reduce-scatter.2.cloned.1.call-update) | async-done | bytes 1048592 | tf_op jit(solution)/shard_map/reduce_scatter | solution.py:61
  521.4 2.4 fusion.24
  (48 shorter events, 8.6 us)
Async XLA Ops:
  6.5 131.9 %all-gather.2.cloned.1.call-start = ((), (), s32[]{:S(2)}) async-start(), calls=%async_computation.1 | async-start | bytes 9437184 | tf_op jit(solution)/shard_map/all_gather | solution.py:23
  10.6 17.2 %copy-start.5 = (f32[16,512]{1,0:T(8,128)S(1)}, f32[16,512]{1,0:T(8,128)}, u32[]{:S(2)}) copy-start(f32[16,512]{1,0:T(8,128)} %param.12) | copy-start | bytes 98308
  10.6 17.3 %copy-start.4 = (f32[16,512]{1,0:T(8,128)S(1)}, f32[16,512]{1,0:T(8,128)}, u32[]{:S(2)}) copy-start(f32[16,512]{1,0:T(8,128)} %param.13) | copy-start | bytes 98308
  10.6 17.4 %copy-start.6 = (f32[3,3,512]{2,1,0:T(4,128)S(1)}, f32[3,3,512]{2,1,0:T(4,128)}, u32[]{:S(2)}) copy-start(f32[3,3,512]{2,1,0:T(4,128)} %param.11) | copy-start | bytes 55300
  10.7 510.7 %reduce-scatter.2.cloned.1.call-start = ((), (), s32[]{:S(2)}) async-start(), calls=%async_computation.2 | async-start | bytes 9437184 | tf_op jit(solution)/shard_map/reduce_scatter | solution.py:61
  28.1 110.3 %copy-start.2 = (f32[16,512]{0,1:T(8,128)}, f32[16,512]{0,1:T(8,128)S(1)}, u32[]{:S(2)}) copy-start(f32[16,512]{0,1:T(8,128)S(1)} %copy.51) | copy-start | bytes 98308
  157.3 2.4 collective-permute-start
  162.6 2.7 copy-start
  165.3 3.9 copy-start.8
  169.3 21.5 %copy-start.3 = (f32[128,512]{0,1:T(8,128)S(1)}, f32[128,512]{0,1:T(8,128)}, u32[]{:S(2)}) copy-start(f32[128,512]{0,1:T(8,128)} %multiply_reduce_fusion) | copy-start | bytes 786436
  179.5 5.4 %collective-permute-start.1 = (bf16[8,16,512]{2,1,0:T(8,128)(2,1)S(1)}, bf16[8,16,512]{2,1,0:T(8,128)(2,1)S(1)}, u32[]{:S(2)}, u32[]{:S(2)}) collective-permute-start(bf16[8,16,512]{2,1,0:T(8,128)(2,1)S(1)} %fusion.25), channel_id=1, source_target_pairs={{0,1},{1,2},{2,3},{4,5},{5,6},{6,7},{8,9},{9,10},{10,11},{12,13},{... | collective-permute-start | bytes 393224 | tf_op jit(solution)/shard_map/ppermute | solution.py:10
  185.7 105.1 %collective-permute-start.2 = (bf16[8,16,512]{2,1,0:T(8,128)(2,1)}, bf16[8,16,512]{2,1,0:T(8,128)(2,1)S(1)}, u32[]{:S(2)}, u32[]{:S(2)}) collective-permute-start(bf16[8,16,512]{2,1,0:T(8,128)(2,1)} %fusion.26), channel_id=1, source_target_pairs={{0,1},{1,2},{2,3},{4,5},{5,6},{6,7},{8,9},{9,10},{10,11},{12,13},{... | collective-permute-start | bytes 393224 | tf_op jit(solution)/shard_map/ppermute | solution.py:10
  290.8 63.0 %collective-permute-start.3 = (bf16[8,16,512]{2,1,0:T(8,128)(2,1)S(1)}, bf16[8,16,512]{2,1,0:T(8,128)(2,1)S(1)}, u32[]{:S(2)}, u32[]{:S(2)}) collective-permute-start(bf16[8,16,512]{2,1,0:T(8,128)(2,1)S(1)} %fusion.27), channel_id=1, source_target_pairs={{0,1},{1,2},{2,3},{4,5},{5,6},{6,7},{8,9},{9,10},{10,11},{12,13},{... | collective-permute-start | bytes 393224 | tf_op jit(solution)/shard_map/ppermute | solution.py:10
  354.6 8.7 %copy-start.7 = (f32[512]{0:T(512)S(1)}, f32[512]{0:T(512)}, u32[]{:S(2)}) copy-start(f32[512]{0:T(512)} %param.14) | copy-start | bytes 6148
  363.3 4.9 copy-start.9
  374.9 146.5 %copy-start.1 = (bf16[1,128,4096]{2,1,0:T(8,128)(2,1)S(1)}, bf16[1,128,4096]{2,1,0:T(8,128)(2,1)}, u32[]{:S(2)}) copy-start(bf16[1,128,4096]{2,1,0:T(8,128)(2,1)} %param.8) | copy-start | bytes 3145732
Sparse Core Ops, SparseCore 0:
  10.7 127.6 all-gather.1
  375.0 146.2 reduce-scatter.1
where the time goes:
time: 532 us; the launch traced here: 531 us
  waiting for transfers between devices  251 us (47%)
  local copies, waits for them, and re-layouts  131 us (25%)
  matrix products  95.2 us (18%)
  other arithmetic  24.1 us (5%)
  starting transfers between devices  15.7 us (3%)
  between operations  13.7 us (3%)
    reduce_scatter x1, waiting for transfers between devices, shards(): lax.psum_scatter(jnp.dot(gated, w_out, preferred_element_type=jnp.float32...  146 us
    all_gather x1, waiting for transfers between devices, shards(): lax.all_gather(normed, 'fsdp', axis=0, tiled=True)  104 us
    gather x2, local copies, waits for them, and re-layouts, shards(): kernel[jnp.maximum(lag_steps, 0)]  99.8 us
    dot_general x1, matrix products, shards(): inside = jnp.einsum('tsc,gsc->gtc', toeplitz, product, precision=high)  56.5 us
    unnamed x22, local copies, waits for them, and re-layouts  19.9 us
    dot_general x1, matrix products, shards(): jnp.einsum('gtd,de->gte', lax.all_gather(normed, 'fsdp', axis=0, tiled=Tr...  18.3 us
    ppermute x4, starting transfers between devices, from_behind(): lax.ppermute(value, axis, [(source, source + steps) for source in range(f...  15.6 us
  transfers between devices with their start and end apart: 6, of which 4 were waited for; matrix products, arithmetic and copies ran while one was open for 34% of the time, Pallas kernels for 0%

commit v1 on v0

v1 whole, which is shorter than its diff:
```python
import jax
import jax.numpy as jnp
from jax import lax
from jax.experimental import pallas as pl
from jax.experimental.pallas import tpu as pltpu
from jax.sharding import PartitionSpec as P


def from_behind(value, axis, steps):
    count = lax.axis_size(axis)
    first, last = (max(0, -steps), min(count, count - steps))
    return lax.ppermute(value, axis, [(source, source + steps) for source in range(first, last)])


LANES = 128


def summary_kernel(decay_ref, product_ref, out_ref):
    poles, groups, lanes = out_ref.shape
    decay = jnp.broadcast_to(jnp.exp(-decay_ref[...])[:, None, :], (poles, groups, lanes))

    def step(t, state):
        return decay * state + product_ref[t][None]

    out_ref[...] = lax.fori_loop(0, product_ref.shape[0], step, jnp.zeros(out_ref.shape, jnp.float32))


def filter_kernel(decay_ref, residues_ref, skip_ref, product_ref, query_ref, incoming_ref, out_ref):
    poles, groups, lanes = incoming_ref.shape
    decay = jnp.broadcast_to(jnp.exp(-decay_ref[...])[:, None, :], (poles, groups, lanes))
    residues = residues_ref[...][:, None, :]
    skip = skip_ref[...]

    def step(t, state):
        product = product_ref[t]
        state = decay * state + product[None]
        out_ref[t] = query_ref[t] * (skip * product + jnp.sum(residues * state, axis=0))
        return state

    lax.fori_loop(0, product_ref.shape[0], step, incoming_ref[...])


def shards(tokens, norm_gain, w_in, taps, decay_rate, residues, skip_gain, w_out):
    values = tokens.astype(jnp.float32)
    inverse_rms = lax.rsqrt(jnp.mean(values * values, axis=-1, keepdims=True) + 1e-06)
    normed = (values * inverse_rms * norm_gain).astype(jnp.bfloat16)
    model_width = w_in.shape[0]
    channels = w_in.shape[2]
    w_flat = w_in.reshape(model_width, 3 * channels)
    features = jnp.einsum(
        "gtd,de->gte",
        lax.all_gather(normed, "fsdp", axis=0, tiled=True),
        w_flat,
        preferred_element_type=jnp.float32,
    ).astype(jnp.bfloat16)
    groups = features.shape[0]
    length = features.shape[1]
    poles = decay_rate.shape[0]
    edge_rows = from_behind(features[:, length - 2 :], "ctx", 1)
    extended = jnp.concatenate([edge_rows, features], axis=1).transpose(1, 0, 2).astype(jnp.float32)
    tap_rows = taps.reshape(taps.shape[0], 3 * channels)
    filtered = tap_rows[0] * extended[2:] + tap_rows[1] * extended[1:-1] + tap_rows[2] * extended[:-2]
    query_part = filtered[:, :, :channels]
    product = filtered[:, :, channels : 2 * channels] * filtered[:, :, 2 * channels :]
    pole_spec = pl.BlockSpec((poles, LANES), lambda c: (0, c))
    state_spec = pl.BlockSpec((poles, groups, LANES), lambda c: (0, 0, c))
    rows_spec = pl.BlockSpec((length, groups, LANES), lambda c: (0, 0, c))
    summary = pl.pallas_call(
        summary_kernel,
        grid=(channels // LANES,),
        in_specs=[pole_spec, rows_spec],
        out_specs=state_spec,
        out_shape=jax.ShapeDtypeStruct((poles, groups, channels), jnp.float32),
    )(decay_rate, product)
    decay_all = jnp.exp(-decay_rate * length)[:, None, :]
    incoming = jnp.zeros_like(summary)
    for hop_step in range(lax.axis_size("ctx") - 1):
        incoming = from_behind(
            (decay_all * incoming + summary).astype(jnp.bfloat16), "ctx", 1
        ).astype(jnp.float32)
    gated = pl.pallas_call(
        filter_kernel,
        grid=(channels // LANES,),
        in_specs=[pole_spec, pole_spec, pl.BlockSpec((1, LANES), lambda c: (0, c)), rows_spec, rows_spec, state_spec],
        out_specs=rows_spec,
        out_shape=jax.ShapeDtypeStruct((length, groups, channels), jnp.float32),
    )(decay_rate, residues, skip_gain[None], product, query_part, incoming)
    gated = gated.astype(jnp.bfloat16).transpose(1, 0, 2).reshape(groups * length, channels)
    summed = lax.psum_scatter(
        jnp.dot(gated, w_out, preferred_element_type=jnp.float32).astype(jnp.bfloat16),
        "fsdp",
        scatter_dimension=0,
        tiled=True,
    ).astype(jnp.float32)
    return (values[0] + summed).astype(jnp.bfloat16)[None]


def solution(mesh):
    in_specs = (
        P("fsdp", "ctx", None),
        P(),
        P(None, None, "fsdp"),
        P(None, None, "fsdp"),
        P(None, "fsdp"),
        P(None, "fsdp"),
        P("fsdp"),
        P("fsdp", None),
    )
    out_specs = P("fsdp", "ctx", None)
    return jax.shard_map(shards, mesh=mesh, in_specs=in_specs, out_specs=out_specs, check_vma=False)
```

time: 532 us -> 380 us (0.71)
  local copies, waits for them, and re-layouts: 131 us -> 17.4 us
  matrix products: 95.2 us -> 28.7 us
  Pallas kernels: 0 us -> 19.8 us
  waiting for transfers between devices: 251 us -> 266 us
  other arithmetic: 24.1 us -> 17.4 us
    gather x2 -> x0, local copies, waits for them, and re-layouts: 99.8 us -> none  [shards(): kernel[jnp.maximum(lag_steps, 0)]]
    dot_general x3 -> x0, matrix products: 70.3 us -> none  [the longest x1 56.5 us: shards(): inside = jnp.einsum('tsc,gsc->gtc', toeplitz, product, precision=high)]
    pallas_call x0 -> x2, Pallas kernels: none -> 19.8 us  [the longest x1 13.9 us: shards(): pl.pallas_call(filter_kernel, grid=(channels // LANES,), in_specs=[pole_s...]
    dot_general x3 -> x0, local copies, waits for them, and re-layouts: 7.02 us -> none  [the longest x1 2.93 us: shards(): entering = jnp.einsum('ntc,gnc->gtc', enter, incoming, precision=high)]
    all_gather x1, waiting for transfers between devices: 104 us -> 111 us  [shards(): lax.all_gather(normed, 'fsdp', axis=0, tiled=True)]
    reduce_sum x1 -> x0, other arithmetic: 6.67 us -> none  [shards(): kernel = jnp.sum(residues[:, None, :] * powers, axis=0)]
    unnamed x22 -> x7, local copies, waits for them, and re-layouts: 19.9 us -> 17.1 us
  transfers between devices with their start and end apart: 6 -> 6, of which waited for: 4 -> 6; matrix products, arithmetic and copies ran while one was open for 34% -> 5% of each run, Pallas kernels for 0% -> 0%
where the time goes in v1:
time: 380 us; the launch traced here: 379 us
  waiting for transfers between devices  266 us (70%)
  matrix products  28.7 us (8%)
  Pallas kernels  19.8 us (5%)
  other arithmetic  17.4 us (5%)
  local copies, waits for them, and re-layouts  17.4 us (5%)
  starting transfers between devices  16.5 us (4%)
  between operations  13.5 us (4%)
    reduce_scatter x1, waiting for transfers between devices, shards(): lax.psum_scatter(jnp.dot(gated, w_out, preferred_element_type=jnp.float32...  152 us
    all_gather x1, waiting for transfers between devices, shards(): lax.all_gather(normed, 'fsdp', axis=0, tiled=True)  111 us
    dot_general x1, matrix products, shards(): jnp.einsum('gtd,de->gte', lax.all_gather(normed, 'fsdp', axis=0, tiled=Tr...  19.8 us
    unnamed x7, local copies, waits for them, and re-layouts  17.1 us
    ppermute x4, starting transfers between devices, from_behind(): lax.ppermute(value, axis, [(source, source + steps) for source in range(f...  16.4 us
    pallas_call x1, Pallas kernels, shards(): pl.pallas_call(filter_kernel, grid=(channels // LANES,), in_specs=[pole_s...  13.9 us
    dot_general x1, matrix products, shards(): jnp.dot(gated, w_out, preferred_element_type=jnp.float32)  8.89 us
  transfers between devices with their start and end apart: 6, of which 6 were waited for; matrix products, arithmetic and copies ran while one was open for 5% of the time, Pallas kernels for 0%

profile of v1, /device:TPU:0, one launch (start us, length us, event | category | flops | bytes accessed | tf_op | source)
XLA Modules:
  0.0 379.1 jit_solution(16935476040335585478)
XLA Ops:
  6.5 1.5 fusion.9
  8.1 2.5 fusion.11
  10.7 17.1 %copy.14 = bf16[4096,3,512]{0,2,1:T(8,128)(2,1)} copy(bf16[4096,3,512]{2,0,1:T(8,128)(2,1)} %param.10) | data formatting | bytes 25165824 | tf_op args[2]
  27.8 110.6 %all-gather.2.cloned.1.call-done = bf16[8,128,4096]{2,1,0:T(8,128)(2,1)} async-done(((bf16[1,128,4096]{2,1,0:T(8,128)(2,1)}), bf16[8,128,4096]{2,1,0:T(8,128)(2,1)}) %all-gather.2.cloned.1.call-update) | async-done | bytes 8388624 | tf_op jit(solution)/shard_map/all_gather | solution.py:52
  138.4 19.8 %fusion.4 = bf16[8,128,1536]{2,0,1:T(8,128)(2,1)S(1)} fusion(bf16[4096,1536,1]{0,1,2:T(8,128)(2,1)} %bitcast.22, bf16[8,128,4096]{2,1,0:T(8,128)(2,1)} %all-gather.2.cloned.1.call-done), kind=kOutput, calls=%fused_computation.9 | convolution fusion | flops 12886474752 | bytes 24117248 | tf_op jit(solution)/shard_map/gtd,de->gte/dot_general | solution.py:50
  158.3 1.3 collective-permute-start
  159.7 0.8 collective-permute-done
  160.9 2.4 fusion.2
  163.3 2.7 fusion.13
  165.9 5.9 %shard_map.82 = f32[16,8,512]{2,1,0:T(8,128)} custom-call(f32[16,512]{1,0:T(8,128)} %decay_ref.3, f32[128,8,512]{2,1,0:T(8,128)} %get-tuple-element.6.product_ref), custom_call_target="tpu_custom_call" | custom-call | tf_op jit(solution)/shard_map/pallas_call | solution.py:68
  171.8 1.0 add_convert_fusion.2
  172.8 4.4 %collective-permute-start.1 = (bf16[16,8,512]{2,1,0:T(8,128)(2,1)S(1)}, bf16[16,8,512]{2,1,0:T(8,128)(2,1)S(1)}, u32[]{:S(2)}, u32[]{:S(2)}) collective-permute-start(bf16[16,8,512]{2,1,0:T(8,128)(2,1)S(1)} %add_convert_fusion.2), channel_id=1, source_target_pairs={{0,1},{1,2},{2,3},{4,5},{5,6},{6,7},{8,9},{9,10},{10,11},{12,13},{... | collective-permute-start | bytes 393224 | tf_op jit(solution)/shard_map/ppermute | solution.py:12
  177.2 1.0 collective-permute-done.1
  178.2 1.0 add_convert_fusion.1
  179.2 5.2 %collective-permute-start.2 = (bf16[16,8,512]{2,1,0:T(8,128)(2,1)S(1)}, bf16[16,8,512]{2,1,0:T(8,128)(2,1)S(1)}, u32[]{:S(2)}, u32[]{:S(2)}) collective-permute-start(bf16[16,8,512]{2,1,0:T(8,128)(2,1)S(1)} %add_convert_fusion.1), channel_id=1, source_target_pairs={{0,1},{1,2},{2,3},{4,5},{5,6},{6,7},{8,9},{9,10},{10,11},{12,13},{... | collective-permute-start | bytes 393224 | tf_op jit(solution)/shard_map/ppermute | solution.py:12
  184.4 1.0 collective-permute-done.2
  185.3 1.0 add_convert_fusion
  186.3 5.5 %collective-permute-start.3 = (bf16[16,8,512]{2,1,0:T(8,128)(2,1)S(1)}, bf16[16,8,512]{2,1,0:T(8,128)(2,1)S(1)}, u32[]{:S(2)}, u32[]{:S(2)}) collective-permute-start(bf16[16,8,512]{2,1,0:T(8,128)(2,1)S(1)} %add_convert_fusion), channel_id=1, source_target_pairs={{0,1},{1,2},{2,3},{4,5},{5,6},{6,7},{8,9},{9,10},{10,11},{12,13},{... | collective-permute-start | bytes 393224 | tf_op jit(solution)/shard_map/ppermute | solution.py:12
  191.8 0.8 collective-permute-done.3
  193.4 13.9 %shard_map.83 = f32[128,8,512]{2,1,0:T(8,128)} custom-call(f32[16,512]{1,0:T(8,128)} %decay_ref.3, f32[16,512]{1,0:T(8,128)} %residues_ref.1, f32[1,512]{1,0:T(1,128)} %bitcast.24, f32[128,8,512]{2,1,0:T(8,128)} %get-tuple-element.6.product_ref, f32[128,8,512]{2,1,0:T(8,128)} %get-tuple-element.5.query_ref, f32[16,8,512]{2,1,0:T(8,128)} %convert_element_type.55.incoming_ref), custom_call_target="tpu_custom_call" | custom-call | tf_op jit(solution)/shard_map/pallas_call | solution.py:81
  207.2 1.7 convert_bitcast_fusion.2
  209.3 8.9 %convolution_convert_fusion = bf16[1024,4096]{1,0:T(8,128)(2,1)} fusion(bf16[1024,512]{1,0:T(8,128)(2,1)S(1)} %bitcast.23, bf16[512,4096]{1,0:T(8,128)(2,1)} %param.15), kind=kOutput, calls=%fused_computation.2 | convolution fusion | flops 4299161600 | bytes 13631488 | tf_op jit(solution)/shard_map/dot_general | solution.py:90
  218.2 151.6 %reduce-scatter.2.cloned.1.call-done = bf16[128,4096]{1,0:T(8,128)(2,1)} async-done(((bf16[1024,4096]{1,0:T(8,128)(2,1)}), bf16[128,4096]{1,0:T(8,128)(2,1)}) %reduce-scatter.2.cloned.1.call-update) | async-done | bytes 1048592 | tf_op jit(solution)/shard_map/reduce_scatter | solution.py:89
  369.8 2.4 fusion.12
  (20 shorter events, 1.6 us)
Async XLA Ops:
  6.5 131.9 %all-gather.2.cloned.1.call-start = ((), (), s32[]{:S(2)}) async-start(), calls=%async_computation.1 | async-start | bytes 9437184 | tf_op jit(solution)/shard_map/all_gather | solution.py:52
  10.6 17.1 %copy-start.1 = (f32[16,512]{1,0:T(8,128)S(1)}, f32[16,512]{1,0:T(8,128)}, u32[]{:S(2)}) copy-start(f32[16,512]{1,0:T(8,128)} %decay_ref.3) | copy-start | bytes 98308
  10.6 359.2 %reduce-scatter.2.cloned.1.call-start = ((), (), s32[]{:S(2)}) async-start(), calls=%async_computation.2 | async-start | bytes 9437184 | tf_op jit(solution)/shard_map/reduce_scatter | solution.py:89
  138.4 21.2 %copy-start.2 = (f32[3,3,512]{2,1,0:T(4,128)S(1)}, f32[3,3,512]{2,1,0:T(4,128)}, u32[]{:S(2)}) copy-start(f32[3,3,512]{2,1,0:T(4,128)} %param.11) | copy-start | bytes 55300
  158.3 2.2 collective-permute-start
  172.8 5.3 %collective-permute-start.1 = (bf16[16,8,512]{2,1,0:T(8,128)(2,1)S(1)}, bf16[16,8,512]{2,1,0:T(8,128)(2,1)S(1)}, u32[]{:S(2)}, u32[]{:S(2)}) collective-permute-start(bf16[16,8,512]{2,1,0:T(8,128)(2,1)S(1)} %add_convert_fusion.2), channel_id=1, source_target_pairs={{0,1},{1,2},{2,3},{4,5},{5,6},{6,7},{8,9},{9,10},{10,11},{12,13},{... | collective-permute-start | bytes 393224 | tf_op jit(solution)/shard_map/ppermute | solution.py:12
  179.2 6.2 %collective-permute-start.2 = (bf16[16,8,512]{2,1,0:T(8,128)(2,1)S(1)}, bf16[16,8,512]{2,1,0:T(8,128)(2,1)S(1)}, u32[]{:S(2)}, u32[]{:S(2)}) collective-permute-start(bf16[16,8,512]{2,1,0:T(8,128)(2,1)S(1)} %add_convert_fusion.1), channel_id=1, source_target_pairs={{0,1},{1,2},{2,3},{4,5},{5,6},{6,7},{8,9},{9,10},{10,11},{12,13},{... | collective-permute-start | bytes 393224 | tf_op jit(solution)/shard_map/ppermute | solution.py:12
  186.3 6.3 %collective-permute-start.3 = (bf16[16,8,512]{2,1,0:T(8,128)(2,1)S(1)}, bf16[16,8,512]{2,1,0:T(8,128)(2,1)S(1)}, u32[]{:S(2)}, u32[]{:S(2)}) collective-permute-start(bf16[16,8,512]{2,1,0:T(8,128)(2,1)S(1)} %add_convert_fusion), channel_id=1, source_target_pairs={{0,1},{1,2},{2,3},{4,5},{5,6},{6,7},{8,9},{9,10},{10,11},{12,13},{... | collective-permute-start | bytes 393224 | tf_op jit(solution)/shard_map/ppermute | solution.py:12
  218.2 151.6 %copy-start = (bf16[1,128,4096]{2,1,0:T(8,128)(2,1)S(1)}, bf16[1,128,4096]{2,1,0:T(8,128)(2,1)}, u32[]{:S(2)}) copy-start(bf16[1,128,4096]{2,1,0:T(8,128)(2,1)} %param.8) | copy-start | bytes 3145732
Sparse Core Ops, SparseCore 0:
  10.7 127.6 all-gather.1
  218.3 151.4 reduce-scatter.1

commit v2 on v1

--- a/solution.py
+++ b/solution.py
@@ -1,3 +1,5 @@
+import functools
+
 import jax
 import jax.numpy as jnp
 from jax import lax
@@ -95,6 +97,414 @@
     return (values[0] + summed).astype(jnp.bfloat16)[None]
 
 
+CHUNKS = 4
+COLUMNS = 256
+STRIP = 16
+UNROLL = 4
+VMEM_BUDGET = 52 * 1024 * 1024
+VMEM_LIMIT = 63 * 1024 * 1024
+
+
+def fused_kernel(
+    nz, nctx,
+    tok, gain, w_in, taps, decay, residues, skip, w_out,
+    out,
+    w_v, wo_v, gat, part, rxx, rz, feat, prod, query, gated, gated_rows, edge_rx, st_tx, st_rx, inc, acc,
+    w_sem, ag_send, ag_recv, x_send, x_recv, z_send, z_recv, edge_send, edge_recv, st_send, st_recv,
+):
+    T, D = tok.shape
+    C = w_in.shape[2]
+    J = C // LANES
+    R = 2 * J
+    NP = decay.shape[0]
+    TC = T // CHUNKS
+    f = lax.axis_index("fsdp")
+    c = lax.axis_index("ctx")
+    z = lax.div(f, 2)
+    x = lax.rem(f, 2)
+    partner = z * 2 + 1 - x
+    has_left, has_right = z > 0, z < nz - 1
+
+    w_copy = pltpu.make_async_copy(w_in, w_v, w_sem.at[0])
+    wo_copy = pltpu.make_async_copy(w_out, wo_v, w_sem.at[1])
+    w_copy.start()
+    wo_copy.start()
+
+    barrier = pltpu.get_barrier_semaphore()
+    pl.semaphore_signal(barrier, inc=1, device_id={"fsdp": partner}, device_id_type=pl.DeviceIdType.MESH)
+
+    @pl.when(has_left)
+    def _():
+        pl.semaphore_signal(barrier, inc=1, device_id={"fsdp": f - 2}, device_id_type=pl.DeviceIdType.MESH)
+
+    @pl.when(has_right)
+    def _():
+        pl.semaphore_signal(barrier, inc=1, device_id={"fsdp": f + 2}, device_id_type=pl.DeviceIdType.MESH)
+
+    for d in range(1, nctx):
+        pl.semaphore_signal(
+            barrier, inc=1, device_id={"ctx": lax.rem(c + d, nctx)}, device_id_type=pl.DeviceIdType.MESH
+        )
+
+    def rows(start, size):
+        return pl.ds(pl.multiple_of(start, STRIP), size)
+
+    @pl.loop(0, T // STRIP)
+    def _(k):
+        value = tok[rows(k * STRIP, STRIP), :].astype(jnp.float32)
+        scale = lax.rsqrt(jnp.mean(value * value, axis=-1, keepdims=True) + 1e-06)
+        gat[rows(f * T + k * STRIP, STRIP), :] = (value * scale * gain[...]).astype(jnp.bfloat16)
+
+    pl.semaphore_wait(barrier, nctx + has_left.astype(jnp.int32) + has_right.astype(jnp.int32))
+
+    def remote(src, dst, send, recv, device):
+        return pltpu.make_async_remote_copy(
+            src_ref=src, dst_ref=dst, send_sem=send, recv_sem=recv,
+            device_id=device, device_id_type=pl.DeviceIdType.MESH,
+        )
+
+    X, UP, DOWN = 0, 1, 2
+
+    def ag(block, ch, way):
+        where = gat.at[rows(block * T + ch * TC, TC), :]
+        target = {X: partner, UP: f + 2, DOWN: f - 2}[way]
+        return remote(
+            where, where, ag_send.at[way, lax.div(block, 2), ch], ag_recv.at[block, ch], {"fsdp": target}
+        )
+
+    def part_x(p, ch):
+        return remote(
+            part.at[rows((p * 2 + 1 - x) * T + ch * TC, TC), :],
+            rxx.at[rows(p * T + ch * TC, TC), :],
+            x_send.at[p, ch], x_recv.at[p, ch], {"fsdp": partner},
+        )
+
+    def part_z(p, ch, slot, target):
+        return remote(
+            part.at[rows((p * 2 + x) * T + ch * TC, TC), :],
+            rz.at[rows(slot * T + ch * TC, TC), :],
+            z_send.at[p, ch], z_recv.at[slot, ch], {"fsdp": target},
+        )
+
+    for ch in range(CHUNKS):
+        ag(f, ch, X).start()
+
+        @pl.when(has_right)
+        def _():
+            ag(f, ch, UP).start()
+
+        @pl.when(has_left)
+        def _():
+            ag(f, ch, DOWN).start()
+
+    def compute(p):
+        @pl.loop(0, CHUNKS)
+        def _(ch):
+            ag(p * 2 + 1 - x, ch, X).wait_recv()
+
+        for i in range(3):
+            for n in range(C // COLUMNS):
+                result = jnp.dot(
+                    gat[rows(p * 2 * T, 2 * T), :],
+                    w_v[i, :, n * COLUMNS : (n + 1) * COLUMNS],
+                    preferred_element_type=jnp.float32,
+                ).astype(jnp.bfloat16).astype(jnp.float32)
+                for s in range(2):
+                    for j in range(COLUMNS // LANES):
+                        first = 2 * R + s * J + n * (COLUMNS // LANES) + j
+                        feat[i, pl.ds(first, T, stride=R), :] = result[
+                            s * T : (s + 1) * T, j * LANES : (j + 1) * LANES
+                        ]
+
+        edge = remote(
+            feat.at[:, pl.ds(T * R, 2 * R), :], edge_rx.at[p], edge_send.at[p], edge_recv.at[p], {"ctx": c + 1}
+        )
+
+        @pl.when(c + 1 < nctx)
+        def _():
+            edge.start()
+
+        @pl.when(c > 0)
+        def _():
+            edge.wait_recv()
+            feat[:, 0 : 2 * R, :] = edge_rx[p]
+
+        @pl.when(c == 0)
+        def _():
+            feat[:, 0 : 2 * R, :] = jnp.zeros((3, 2 * R, LANES), jnp.float32)
+
+        def first_pass(block, state):
+            decays = [jnp.exp(-decay[n]) for n in range(NP)]
+            for k in range(UNROLL):
+                base = (block * UNROLL + k) * R
+                filtered = [
+                    taps[0, i] * feat[i, pl.ds(pl.multiple_of(base + 2 * R, R), R), :]
+                    + taps[1, i] * feat[i, pl.ds(pl.multiple_of(base + R, R), R), :]
+                    + taps[2, i] * feat[i, pl.ds(pl.multiple_of(base, R), R), :]
+                    for i in range(3)
+                ]
+                product = filtered[1] * filtered[2]
+                prod[pl.ds(pl.multiple_of(base, R), R), :] = product
+                query[pl.ds(pl.multiple_of(base, R), R), :] = filtered[0]
+                state = tuple(decays[n] * state[n] + product for n in range(NP))
+            return state
+
+        zero = jnp.zeros((R, LANES), jnp.float32)
+        state = lax.fori_loop(0, T // UNROLL, first_pass, (zero,) * NP)
+        for n in range(NP):
+            st_tx[p, n] = state[n]
+
+        def state_copy(d):
+            return remote(
+                st_tx.at[p], st_rx.at[p, d - 1], st_send.at[p, d - 1], st_recv.at[p, d - 1], {"ctx": c + d}
+            )
+
+        for d in range(1, nctx):
+            @pl.when(c + d < nctx)
+            def _():
+                state_copy(d).start()
+
+        inc[...] = jnp.zeros(inc.shape, jnp.float32)
+        for d in range(1, nctx):
+            @pl.when(c >= d)
+            def _():
+                state_copy(d).wait_recv()
+                inc[...] += jnp.exp(decay[...] * (-float(T * (d - 1)))) * st_rx[p, d - 1]
+
+        def second_pass(block, state):
+            decays = [jnp.exp(-decay[n]) for n in range(NP)]
+            for k in range(UNROLL):
+                here = pl.ds(pl.multiple_of((block * UNROLL + k) * R, R), R)
+                product = prod[here, :]
+                state = tuple(decays[n] * state[n] + product for n in range(NP))
+                sums = [skip[...] * product] + [residues[n] * state[n] for n in range(NP)]
+                while len(sums) > 1:
+                    sums = [sum(sums[k : k + 2]) for k in range(0, len(sums), 2)]
+                gated[here, :] = query[here, :] * sums[0]
+            return state
+
+        lax.fori_loop(0, T // UNROLL, second_pass, tuple(inc[n] for n in range(NP)))
+        for s in range(2):
+            for j in range(J):
+                gated_rows[s * T : (s + 1) * T, j * LANES : (j + 1) * LANES] = gated[
+                    pl.ds(s * J + j, T, stride=R), :
+                ].astype(jnp.bfloat16)
+
+        @pl.loop(0, D // COLUMNS)
+        def _(n):
+            where = pl.ds(pl.multiple_of(n * COLUMNS, COLUMNS), COLUMNS)
+            part[rows(p * 2 * T, 2 * T), where] = jnp.dot(
+                gated_rows[...], wo_v[:, where], preferred_element_type=jnp.float32
+            ).astype(jnp.bfloat16)
+
+        @pl.loop(0, CHUNKS)
+        def _(ch):
+            part_x(p, ch).start()
+
+        @pl.when(c + 1 < nctx)
+        def _():
+            edge.wait_send()
+
+        for d in range(1, nctx):
+            @pl.when(c + d < nctx)
+            def _():
+                state_copy(d).wait_send()
+
+    w_copy.wait()
+    wo_copy.wait()
+
+    def main_step(h, carry):
+        @pl.when(h < nz)
+        def _():
+            @pl.loop(0, CHUNKS)
+            def _(ch):
+                @pl.when(z - h >= 0)
+                def _():
+                    block = (z - h) * 2 + x
+                    ag(block, ch, UP).wait_recv()
+
+                    @pl.when(has_right)
+                    def _():
+                        ag(block, ch, UP).start()
+
+                    ag(block, ch, X).start()
+
+                @pl.when(z + h < nz)
+                def _():
+                    block = (z + h) * 2 + x
+                    ag(block, ch, DOWN).wait_recv()
+
+                    @pl.when(has_left)
+                    def _():
+                        ag(block, ch, DOWN).start()
+
+                    ag(block, ch, X).start()
+
+        def side_step(side, carry):
+            p = z + (h - 1) * (2 * side - 1)
+
+            @pl.when((p >= 0) & (p < nz) & ((h > 1) | (side == 0)))
+            def _():
+                compute(p)
+
+            return carry
+
+        return lax.fori_loop(0, 2, side_step, carry)
+
+    lax.fori_loop(1, nz + 1, main_step, 0)
+
+    def load(ref, start, k):
+        return ref[rows(start + k * STRIP, STRIP), :].astype(jnp.float32)
+
+    def combine(p, ch, more):
+        start = (p * 2 + x) * T + ch * TC
+        other = p * T + ch * TC
+        part_x(p, ch).wait_recv()
+
+        @pl.when(more)
+        def _():
+            part_z(p, ch, p, partner).wait_recv()
+
+            @pl.loop(0, TC // STRIP)
+            def _(k):
+                total = load(part, start, k) + load(rxx, other, k) + load(rz, other, k)
+                part[rows(start + k * STRIP, STRIP), :] = total.astype(jnp.bfloat16)
+
+        @pl.when(jnp.logical_not(more))
+        def _():
+            @pl.loop(0, TC // STRIP)
+            def _(k):
+                total = load(part, start, k) + load(rxx, other, k)
+                part[rows(start + k * STRIP, STRIP), :] = total.astype(jnp.bfloat16)
+
+    def reduce_step(i, carry):
+        down = nz - 1 - i
+
+        @pl.loop(0, CHUNKS)
+        def _(ch):
+            @pl.when(i > z)
+            def _():
+                combine(i, ch, has_left)
+                part_z(i, ch, i, f + 2).start()
+
+            @pl.when(down < z)
+            def _():
+                combine(down, ch, has_right)
+                part_z(down, ch, jnp.where(down == z - 1, nz, down), f - 2).start()
+
+        return carry
+
+    lax.fori_loop(1, nz, reduce_step, 0)
+
+    @pl.loop(0, CHUNKS)
+    def _(ch):
+        start = ch * TC
+        part_x(z, ch).wait_recv()
+
+        @pl.loop(0, TC // STRIP)
+        def _(k):
+            acc[rows(k * STRIP, STRIP), :] = (
+                load(tok, start, k) + load(part, f * T + start, k) + load(rxx, z * T + start, k)
+            )
+
+        for more, slot in ((has_left, z), (has_right, nz)):
+            @pl.when(more)
+            def _():
+                part_z(z, ch, slot, partner).wait_recv()
+
+                @pl.loop(0, TC // STRIP)
+                def _(k):
+                    acc[rows(k * STRIP, STRIP), :] += load(rz, slot * T + start, k)
+
+        @pl.loop(0, TC // STRIP)
+        def _(k):
+            out[rows(start + k * STRIP, STRIP), :] = acc[rows(k * STRIP, STRIP), :].astype(jnp.bfloat16)
+
+    @pl.loop(0, nz)
+    def _(p):
+        @pl.loop(0, CHUNKS)
+        def _(ch):
+            ag(p * 2 + x, ch, X).wait_send()
+            part_x(p, ch).wait_send()
+
+            @pl.when((p <= z) & has_right)
+            def _():
+                ag(p * 2 + x, ch, UP).wait_send()
+
+            @pl.when((p >= z) & has_left)
+            def _():
+                ag(p * 2 + x, ch, DOWN).wait_send()
+
+            @pl.when(p != z)
+            def _():
+                part_z(p, ch, p, partner).wait_send()
+
+
+def scratch_of(nz, nctx, T, D, C, NP):
+    R = 2 * C // LANES
+    f32, bf16 = jnp.float32, jnp.bfloat16
+    arrays = [
+        ((3, D, C), bf16),
+        ((C, D), bf16),
+        ((nz * 2 * T, D), bf16),
+        ((nz * 2 * T, D), bf16),
+        ((nz * T, D), bf16),
+        (((nz + 1) * T, D), bf16),
+        ((3, (T + 2) * R, LANES), f32),
+        ((T * R, LANES), f32),
+        ((T * R, LANES), f32),
+        ((T * R, LANES), f32),
+        ((2 * T, C), bf16),
+        ((nz, 3, 2 * R, LANES), f32),
+        ((nz, NP, R, LANES), f32),
+        ((nz, nctx - 1, NP, R, LANES), f32),
+        ((NP, R, LANES), f32),
+        ((T // CHUNKS, D), f32),
+    ]
+    size = sum(functools.reduce(lambda a, b: a * b, shape) * jnp.dtype(kind).itemsize for shape, kind in arrays)
+    return arrays, size
+
+
+def fused_shards(nz, nctx, tokens, norm_gain, w_in, taps, decay_rate, residues, skip_gain, w_out):
+    T, D = tokens.shape[1:]
+    C = w_in.shape[2]
+    NP = decay_rate.shape[0]
+
+    def twice(value):
+        value = value.reshape(value.shape[:-1] + (C // LANES, LANES))
+        return jnp.concatenate([value, value], axis=-2)
+
+    arrays, _ = scratch_of(nz, nctx, T, D, C, NP)
+    dma = pltpu.SemaphoreType.DMA
+    vmem, anywhere = pl.BlockSpec(memory_space=pltpu.VMEM), pl.BlockSpec(memory_space=pl.ANY)
+    return pl.pallas_call(
+        functools.partial(fused_kernel, nz, nctx),
+        out_shape=jax.ShapeDtypeStruct((T, D), jnp.bfloat16),
+        in_specs=[vmem, vmem, anywhere, vmem, vmem, vmem, vmem, anywhere],
+        out_specs=vmem,
+        scratch_shapes=[pltpu.VMEM(shape, kind) for shape, kind in arrays]
+        + [
+            dma((2,)),
+            dma((3, nz, CHUNKS)),
+            dma((2 * nz, CHUNKS)),
+            dma((nz, CHUNKS)),
+            dma((nz, CHUNKS)),
+            dma((nz, CHUNKS)),
+            dma((nz + 1, CHUNKS)),
+            dma((nz,)),
+            dma((nz,)),
+            dma((nz, nctx - 1)),
+            dma((nz, nctx - 1)),
+        ],
+        compiler_params=pltpu.CompilerParams(
+            collective_id=0, has_side_effects=True, vmem_limit_bytes=VMEM_LIMIT
+        ),
+    )(
+        tokens[0], norm_gain[None], w_in.transpose(1, 0, 2), twice(taps), twice(decay_rate),
+        twice(residues), twice(skip_gain), w_out,
+    )[None]
+
+
 def solution(mesh):
     in_specs = (
         P("fsdp", "ctx", None),
@@ -107,4 +517,18 @@
         P("fsdp", None),
     )
     out_specs = P("fsdp", "ctx", None)
-    return jax.shard_map(shards, mesh=mesh, in_specs=in_specs, out_specs=out_specs, check_vma=False)
+    count, nctx = mesh.shape["fsdp"], mesh.shape["ctx"]
+
+    def whole(tokens, norm_gain, w_in, *rest):
+        D, channels = w_in.shape[0], w_in.shape[2] // count
+        length, poles = tokens.shape[1] // nctx, rest[1].shape[0]
+        _, size = scratch_of(count // 2, nctx, length, D, channels, poles)
+        fits = size <= VMEM_BUDGET and count % 2 == 0 and tokens.shape[0] == count
+        fits = fits and channels % (4 * LANES) == 0 and length % (CHUNKS * STRIP) == 0
+        chosen = functools.partial(fused_shards, count // 2, nctx) if fits else shards
+        return sharded(chosen)(tokens, norm_gain, w_in, *rest)
+
+    def sharded(body):
+        return jax.shard_map(body, mesh=mesh, in_specs=in_specs, out_specs=out_specs, check_vma=False)
+
+    return whole

time: 380 us -> 277 us (0.73)
  waiting for transfers between devices: 266 us -> 0 us
  Pallas kernels: 19.8 us -> 268 us
  matrix products: 28.7 us -> 0 us
  starting transfers between devices: 16.5 us -> 0 us
  other arithmetic: 17.4 us -> 2.65 us
  between operations: 13.5 us -> 0.01 us
  local copies, waits for them, and re-layouts: 17.4 us -> 4.59 us
    pallas_call x2 -> x1, Pallas kernels: 19.8 us -> 268 us  [fused_shards(): pl.pallas_call(functools.partial(fused_kernel, nz, nctx), out_shape=jax.S...]
    reduce_scatter x1 -> x0, waiting for transfers between devices: 152 us -> none  [shards(): lax.psum_scatter(jnp.dot(gated, w_out, preferred_element_type=jnp.float32...]
    all_gather x1 -> x0, waiting for transfers between devices: 111 us -> none  [shards(): lax.all_gather(normed, 'fsdp', axis=0, tiled=True)]
    dot_general x2 -> x0, matrix products: 28.7 us -> none  [the longest x1 19.8 us: shards(): jnp.einsum('gtd,de->gte', lax.all_gather(normed, 'fsdp', axis=0, tiled=Tr...]
    ppermute x4 -> x0, starting transfers between devices: 16.4 us -> none  [from_behind(): lax.ppermute(value, axis, [(source, source + steps) for source in range(f...]
    unnamed x7 -> x1, local copies, waits for them, and re-layouts: 17.1 us -> 2.29 us
    convert_element_type x6 -> x0, other arithmetic: 6.65 us -> none  [the longest x3 2.97 us: shards(): (decay_all * incoming + summary).astype(jnp.bfloat16)]
  transfers between devices with their start and end apart: 6 -> 0, of which waited for: 6 -> 0; matrix products, arithmetic and copies ran while one was open for 5% -> 0% of each run, Pallas kernels for 0% -> 0%
where the time goes in v2:
time: 277 us; the launch traced here: 275 us
  Pallas kernels  268 us (97%)
  local copies, waits for them, and re-layouts  4.59 us (2%)
    pallas_call x1, Pallas kernels, fused_shards(): pl.pallas_call(functools.partial(fused_kernel, nz, nctx), out_shape=jax.S...  268 us

profile of v2, /device:TPU:0, one launch (start us, length us, event | category | flops | bytes accessed | tf_op | source)
XLA Modules:
  0.0 275.1 jit_solution(3893379520445434940)
XLA Ops:
  0.0 1.4 pad_maximum_fusion.3.skip
  1.4 0.8 reshape.12
  2.1 0.6 pad_maximum_fusion.2.taps
  2.7 0.8 reshape.13
  3.5 0.8 reshape.14
  4.3 0.7 pad_maximum_fusion
  5.0 267.8 %shard_map.82 = bf16[128,4096]{1,0:T(8,128)(2,1)} custom-call(bf16[128,4096]{1,0:T(8,128)(2,1)} %bitcast.7, f32[1,4096]{1,0:T(1,128)} %bitcast.8, bf16[3,4096,512]{2,1,0:T(8,128)(2,1)} %bitcast.5, f32[3,3,8,128]{3,2,1,0:T(8,128)} %pad_maximum_fusion.2.taps, f32[16,8,128]{2,1,0:T(8,128)} %get-tuple-element.5.decay, f32[16,8,128]{2,1,0:T(8,128)} %get-tuple-element.6.residues, ...), custom_call_target="tpu_custom_call" | custom-call | tf_op jit(solution)/shard_map/pallas_call | solution.py:480
  272.8 2.3 copy.10

commit v3 on v2

--- a/solution.py
+++ b/solution.py
@@ -107,16 +107,17 @@
 
 def fused_kernel(
     nz, nctx,
-    tok, gain, w_in, taps, decay, residues, skip, w_out,
+    tok, gain, w_in, taps_in, decay_in, residues_in, skip_in, w_out,
     out,
-    w_v, wo_v, gat, part, rxx, rz, feat, prod, query, gated, gated_rows, edge_rx, st_tx, st_rx, inc, acc,
-    w_sem, ag_send, ag_recv, x_send, x_recv, z_send, z_recv, edge_send, edge_recv, st_send, st_recv,
+    w_v, wo_v, gat, part, rxx, rz, feat, prod, query, gated, gated_rows, edge_rx, st_tx, st_rx, inc, acc, rzo,
+    taps, decay, residues, skip,
+    w_sem, ag_send, ag_recv, x_send, x_recv, z_send, z_recv, o_send, o_recv, edge_send, edge_recv, st_send, st_recv,
 ):
     T, D = tok.shape
     C = w_in.shape[2]
     J = C // LANES
     R = 2 * J
-    NP = decay.shape[0]
+    NP = decay_in.shape[0]
     TC = T // CHUNKS
     f = lax.axis_index("fsdp")
     c = lax.axis_index("ctx")
@@ -149,14 +150,6 @@
     def rows(start, size):
         return pl.ds(pl.multiple_of(start, STRIP), size)
 
-    @pl.loop(0, T // STRIP)
-    def _(k):
-        value = tok[rows(k * STRIP, STRIP), :].astype(jnp.float32)
-        scale = lax.rsqrt(jnp.mean(value * value, axis=-1, keepdims=True) + 1e-06)
-        gat[rows(f * T + k * STRIP, STRIP), :] = (value * scale * gain[...]).astype(jnp.bfloat16)
-
-    pl.semaphore_wait(barrier, nctx + has_left.astype(jnp.int32) + has_right.astype(jnp.int32))
-
     def remote(src, dst, send, recv, device):
         return pltpu.make_async_remote_copy(
             src_ref=src, dst_ref=dst, send_sem=send, recv_sem=recv,
@@ -169,7 +162,7 @@
         where = gat.at[rows(block * T + ch * TC, TC), :]
         target = {X: partner, UP: f + 2, DOWN: f - 2}[way]
         return remote(
-            where, where, ag_send.at[way, lax.div(block, 2), ch], ag_recv.at[block, ch], {"fsdp": target}
+            where, where, ag_send.at[way, block, ch], ag_recv.at[block, ch], {"fsdp": target}
         )
 
     def part_x(p, ch):
@@ -187,6 +180,14 @@
         )
 
     for ch in range(CHUNKS):
+        @pl.loop(ch * (TC // STRIP), (ch + 1) * (TC // STRIP))
+        def _(k):
+            value = tok[rows(k * STRIP, STRIP), :].astype(jnp.float32)
+            scale = lax.rsqrt(jnp.mean(value * value, axis=-1, keepdims=True) + 1e-06)
+            gat[rows(f * T + k * STRIP, STRIP), :] = (value * scale * gain[...]).astype(jnp.bfloat16)
+
+        if ch == 0:
+            pl.semaphore_wait(barrier, nctx + has_left.astype(jnp.int32) + has_right.astype(jnp.int32))
         ag(f, ch, X).start()
 
         @pl.when(has_right)
@@ -197,8 +198,29 @@
         def _():
             ag(f, ch, DOWN).start()
 
+    for s in range(2):
+        for j in range(J):
+            row, lanes = s * J + j, slice(j * LANES, (j + 1) * LANES)
+            for n in range(NP):
+                decay[n, row : row + 1, :] = decay_in[n : n + 1, lanes]
+                residues[n, row : row + 1, :] = residues_in[n : n + 1, lanes]
+            for k in range(3):
+                for i in range(3):
+                    taps[k, i, row : row + 1, :] = taps_in[k, i : i + 1, lanes]
+            skip[row : row + 1, :] = skip_in[0:1, lanes]
+
+    ag(partner, 0, X).wait_recv()
+
+    @pl.when(has_right)
+    def _():
+        ag(partner, 0, UP).start()
+
+    @pl.when(has_left)
+    def _():
+        ag(partner, 0, DOWN).start()
+
     def compute(p):
-        @pl.loop(0, CHUNKS)
+        @pl.loop(1, CHUNKS)
         def _(ch):
             ag(p * 2 + 1 - x, ch, X).wait_recv()
 
@@ -297,7 +319,7 @@
                 gated_rows[...], wo_v[:, where], preferred_element_type=jnp.float32
             ).astype(jnp.bfloat16)
 
-        @pl.loop(0, CHUNKS)
+        @pl.loop(1, CHUNKS)
         def _(ch):
             part_x(p, ch).start()
 
@@ -316,28 +338,34 @@
     def main_step(h, carry):
         @pl.when(h < nz)
         def _():
-            @pl.loop(0, CHUNKS)
+            def relay(block, ch, way):
+                ag(block, ch, way).wait_recv()
+
+                @pl.when(has_right if way == UP else has_left)
+                def _():
+                    ag(block, ch, way).start()
+
+            for column in range(2):
+                @pl.when(z - h >= 0)
+                def _():
+                    relay((z - h) * 2 + column, 0, UP)
+
+                @pl.when(z + h < nz)
+                def _():
+                    relay((z + h) * 2 + column, 0, DOWN)
+
+            @pl.loop(1, CHUNKS)
             def _(ch):
                 @pl.when(z - h >= 0)
                 def _():
                     block = (z - h) * 2 + x
-                    ag(block, ch, UP).wait_recv()
-
-                    @pl.when(has_right)
-                    def _():
-                        ag(block, ch, UP).start()
-
+                    relay(block, ch, UP)
                     ag(block, ch, X).start()
 
                 @pl.when(z + h < nz)
                 def _():
                     block = (z + h) * 2 + x
-                    ag(block, ch, DOWN).wait_recv()
-
-                    @pl.when(has_left)
-                    def _():
-                        ag(block, ch, DOWN).start()
-
+                    relay(block, ch, DOWN)
                     ag(block, ch, X).start()
 
         def side_step(side, carry):
@@ -349,9 +377,13 @@
 
             return carry
 
-        return lax.fori_loop(0, 2, side_step, carry)
-
-    lax.fori_loop(1, nz + 1, main_step, 0)
+        lax.fori_loop(0, 2, side_step, 0)
+
+        @pl.when(h > 2)
+        def _():
+            reduce_step(h - 2)
+
+        return carry
 
     def load(ref, start, k):
         return ref[rows(start + k * STRIP, STRIP), :].astype(jnp.float32)
@@ -377,10 +409,47 @@
                 total = load(part, start, k) + load(rxx, other, k)
                 part[rows(start + k * STRIP, STRIP), :] = total.astype(jnp.bfloat16)
 
-    def reduce_step(i, carry):
+    def other_z(p, slot, target):
+        return remote(
+            part.at[rows((p * 2 + 1 - x) * T, TC), :],
+            rzo.at[rows(slot * TC, TC), :],
+            o_send.at[p], o_recv.at[slot], {"fsdp": target},
+        )
+
+    def add_in(start, ref, begin):
+        @pl.loop(0, TC // STRIP)
+        def _(k):
+            total = load(part, start, k) + load(ref, begin, k)
+            part[rows(start + k * STRIP, STRIP), :] = total.astype(jnp.bfloat16)
+
+    def first_chunk(p, more, slot, target):
+        @pl.when(more)
+        def _():
+            part_z(p, 0, p, partner).wait_recv()
+            add_in((p * 2 + x) * T, rz, p * T)
+
+        part_z(p, 0, slot, target).start()
+
+        @pl.when(more)
+        def _():
+            other_z(p, p, partner).wait_recv()
+            add_in((p * 2 + 1 - x) * T, rzo, p * TC)
+
+        other_z(p, slot, target).start()
+
+    def reduce_step(i):
         down = nz - 1 - i
-
-        @pl.loop(0, CHUNKS)
+        down_slot = jnp.where(down == z - 1, nz, down)
+
+        @pl.when(i > z)
+        def _():
+            first_chunk(i, has_left, i, f + 2)
+
+        @pl.when(down < z)
+        def _():
+            first_chunk(down, has_right, down_slot, f - 2)
+
+        @pl.loop(1, CHUNKS)
         def _(ch):
             @pl.when(i > z)
             def _():
@@ -390,14 +459,22 @@
             @pl.when(down < z)
             def _():
                 combine(down, ch, has_right)
-                part_z(down, ch, jnp.where(down == z - 1, nz, down), f - 2).start()
-
-        return carry
-
-    lax.fori_loop(1, nz, reduce_step, 0)
+                part_z(down, ch, down_slot, f - 2).start()
+
+    lax.fori_loop(1, nz + 1, main_step, 0)
+    reduce_step(nz - 1)
+
+    for more, slot in ((has_left, z), (has_right, nz)):
+        @pl.when(more)
+        def _():
+            other_z(z, slot, partner).wait_recv()
+            add_in(partner * T, rzo, slot * TC)
+
+    part_x(z, 0).start()
 
     @pl.loop(0, CHUNKS)
-    def _(ch):
+    def _(turn):
+        ch = lax.rem(turn + 1, CHUNKS)
         start = ch * TC
         part_x(z, ch).wait_recv()
 
@@ -424,8 +501,10 @@
     def _(p):
         @pl.loop(0, CHUNKS)
         def _(ch):
-            ag(p * 2 + x, ch, X).wait_send()
-            part_x(p, ch).wait_send()
+            @pl.when((ch > 0) | (p == z))
+            def _():
+                ag(p * 2 + x, ch, X).wait_send()
+                part_x(p, ch).wait_send()
 
             @pl.when((p <= z) & has_right)
             def _():
@@ -438,6 +517,18 @@
             @pl.when(p != z)
             def _():
                 part_z(p, ch, p, partner).wait_send()
+
+        @pl.when((p <= z) & has_right)
+        def _():
+            ag(p * 2 + 1 - x, 0, UP).wait_send()
+
+        @pl.when((p >= z) & has_left)
+        def _():
+            ag(p * 2 + 1 - x, 0, DOWN).wait_send()
+
+        @pl.when(p != z)
+        def _():
+            other_z(p, p, partner).wait_send()
 
 
 def scratch_of(nz, nctx, T, D, C, NP):
@@ -460,6 +551,11 @@
         ((nz, nctx - 1, NP, R, LANES), f32),
         ((NP, R, LANES), f32),
         ((T // CHUNKS, D), f32),
+        (((nz + 1) * T // CHUNKS, D), bf16),
+        ((3, 3, R, LANES), f32),
+        ((NP, R, LANES), f32),
+        ((NP, R, LANES), f32),
+        ((R, LANES), f32),
     ]
     size = sum(functools.reduce(lambda a, b: a * b, shape) * jnp.dtype(kind).itemsize for shape, kind in arrays)
     return arrays, size
@@ -469,10 +565,6 @@
     T, D = tokens.shape[1:]
     C = w_in.shape[2]
     NP = decay_rate.shape[0]
-
-    def twice(value):
-        value = value.reshape(value.shape[:-1] + (C // LANES, LANES))
-        return jnp.concatenate([value, value], axis=-2)
 
     arrays, _ = scratch_of(nz, nctx, T, D, C, NP)
     dma = pltpu.SemaphoreType.DMA
@@ -485,12 +577,14 @@
         scratch_shapes=[pltpu.VMEM(shape, kind) for shape, kind in arrays]
         + [
             dma((2,)),
-            dma((3, nz, CHUNKS)),
+            dma((3, 2 * nz, CHUNKS)),
             dma((2 * nz, CHUNKS)),
             dma((nz, CHUNKS)),
             dma((nz, CHUNKS)),
             dma((nz, CHUNKS)),
             dma((nz + 1, CHUNKS)),
+            dma((nz,)),
+            dma((nz + 1,)),
             dma((nz,)),
             dma((nz,)),
             dma((nz, nctx - 1)),
@@ -500,8 +594,7 @@
             collective_id=0, has_side_effects=True, vmem_limit_bytes=VMEM_LIMIT
         ),
     )(
-        tokens[0], norm_gain[None], w_in.transpose(1, 0, 2), twice(taps), twice(decay_rate),
-        twice(residues), twice(skip_gain), w_out,
+        tokens[0], norm_gain[None], w_in.transpose(1, 0, 2), taps, decay_rate, residues, skip_gain[None], w_out,
     )[None]
 
 

time: 277 us -> 247 us (0.89)
  Pallas kernels: 268 us -> 243 us
    pallas_call x1, Pallas kernels: 268 us -> 243 us  [fused_shards(): pl.pallas_call(functools.partial(fused_kernel, nz, nctx), out_shape=jax.S...]
where the time goes in v3:
time: 247 us; the launch traced here: 245 us
  Pallas kernels  243 us (98%)
    pallas_call x1, Pallas kernels, fused_shards(): pl.pallas_call(functools.partial(fused_kernel, nz, nctx), out_shape=jax.S...  243 us

profile of v3, /device:TPU:0, one launch (start us, length us, event | category | flops | bytes accessed | tf_op | source)
XLA Modules:
  0.0 244.9 jit_solution(11216558521267749272)
XLA Ops:
  0.0 242.6 %shard_map.82 = bf16[128,4096]{1,0:T(8,128)(2,1)} custom-call(bf16[128,4096]{1,0:T(8,128)(2,1)} %bitcast.7, f32[1,4096]{1,0:T(1,128)} %bitcast.8, bf16[3,4096,512]{2,1,0:T(8,128)(2,1)} %bitcast.5, f32[3,3,512]{2,1,0:T(4,128)} %taps_in.1, f32[16,512]{1,0:T(8,128)} %decay_in.1, f32[16,512]{1,0:T(8,128)} %residues_in.1, f32[1,512]{1,0:T(1,128)} %bitcast.9, ...), custom_call_target="tpu_custom_call" | custom-call | tf_op jit(solution)/shard_map/pallas_call | solution.py:572
  242.6 2.3 copy.10

commit v4 on v3

--- a/solution.py
+++ b/solution.py
@@ -110,7 +110,7 @@
     tok, gain, w_in, taps_in, decay_in, residues_in, skip_in, w_out,
     out,
     w_v, wo_v, gat, part, rxx, rz, feat, prod, query, gated, gated_rows, edge_rx, st_tx, st_rx, inc, acc, rzo,
-    taps, decay, residues, skip,
+    taps, decay, residues, skip, factor,
     w_sem, ag_send, ag_recv, x_send, x_recv, z_send, z_recv, o_send, o_recv, edge_send, edge_recv, st_send, st_recv,
 ):
     T, D = tok.shape
@@ -208,6 +208,7 @@
                 for i in range(3):
                     taps[k, i, row : row + 1, :] = taps_in[k, i : i + 1, lanes]
             skip[row : row + 1, :] = skip_in[0:1, lanes]
+    factor[...] = jnp.exp(-decay[...])
 
     ag(partner, 0, X).wait_recv()
 
@@ -246,6 +247,34 @@
         def _():
             edge.start()
 
+        def filter_row(base):
+            filtered = [
+                taps[0, i] * feat[i, pl.ds(pl.multiple_of(base + 2 * R, R), R), :]
+                + taps[1, i] * feat[i, pl.ds(pl.multiple_of(base + R, R), R), :]
+                + taps[2, i] * feat[i, pl.ds(pl.multiple_of(base, R), R), :]
+                for i in range(3)
+            ]
+            product = filtered[1] * filtered[2]
+            prod[pl.ds(pl.multiple_of(base, R), R), :] = product
+            query[pl.ds(pl.multiple_of(base, R), R), :] = filtered[0]
+            return product
+
+        def first_pass(block, state):
+            decays = [factor[n] for n in range(NP)]
+            for k in range(UNROLL):
+                base = (block * UNROLL + k) * R
+                product = filter_row(base)
+                state = tuple(decays[n] * state[n] + product for n in range(NP))
+            return state
+
+        state = (jnp.zeros((R, LANES), jnp.float32),) * NP
+        for t in range(2, UNROLL):
+            product = filter_row(t * R)
+            state = tuple(factor[n] * state[n] + product for n in range(NP))
+        state = lax.fori_loop(1, T // UNROLL, first_pass, state)
+        for n in range(NP):
+            st_tx[p, n] = state[n]
+
         @pl.when(c > 0)
         def _():
             edge.wait_recv()
@@ -255,26 +284,9 @@
         def _():
             feat[:, 0 : 2 * R, :] = jnp.zeros((3, 2 * R, LANES), jnp.float32)
 
-        def first_pass(block, state):
-            decays = [jnp.exp(-decay[n]) for n in range(NP)]
-            for k in range(UNROLL):
-                base = (block * UNROLL + k) * R
-                filtered = [
-                    taps[0, i] * feat[i, pl.ds(pl.multiple_of(base + 2 * R, R), R), :]
-                    + taps[1, i] * feat[i, pl.ds(pl.multiple_of(base + R, R), R), :]
-                    + taps[2, i] * feat[i, pl.ds(pl.multiple_of(base, R), R), :]
-                    for i in range(3)
-                ]
-                product = filtered[1] * filtered[2]
-                prod[pl.ds(pl.multiple_of(base, R), R), :] = product
-                query[pl.ds(pl.multiple_of(base, R), R), :] = filtered[0]
-                state = tuple(decays[n] * state[n] + product for n in range(NP))
-            return state
-
-        zero = jnp.zeros((R, LANES), jnp.float32)
-        state = lax.fori_loop(0, T // UNROLL, first_pass, (zero,) * NP)
+        early = [filter_row(t * R) for t in range(2)]
         for n in range(NP):
-            st_tx[p, n] = state[n]
+            st_tx[p, n] += (factor[n] * early[0] + early[1]) * jnp.exp(decay[n] * (-float(T - 2)))
 
         def state_copy(d):
             return remote(
@@ -294,7 +306,7 @@
                 inc[...] += jnp.exp(decay[...] * (-float(T * (d - 1)))) * st_rx[p, d - 1]
 
         def second_pass(block, state):
-            decays = [jnp.exp(-decay[n]) for n in range(NP)]
+            decays = [factor[n] for n in range(NP)]
             for k in range(UNROLL):
                 here = pl.ds(pl.multiple_of((block * UNROLL + k) * R, R), R)
                 product = prod[here, :]
@@ -437,29 +449,33 @@
 
         other_z(p, slot, target).start()
 
+    def send_sum(p, ch, more, slot, target):
+        @pl.when(ch == 0)
+        def _():
+            first_chunk(p, more, slot, target)
+
+        @pl.when(ch > 0)
+        def _():
+            combine(p, ch, more)
+            part_z(p, ch, slot, target).start()
+
+    up_late = (2 * z >= nz).astype(jnp.int32)
+
     def reduce_step(i):
         down = nz - 1 - i
         down_slot = jnp.where(down == z - 1, nz, down)
 
-        @pl.when(i > z)
-        def _():
-            first_chunk(i, has_left, i, f + 2)
-
-        @pl.when(down < z)
-        def _():
-            first_chunk(down, has_right, down_slot, f - 2)
-
-        @pl.loop(1, CHUNKS)
-        def _(ch):
-            @pl.when(i > z)
-            def _():
-                combine(i, ch, has_left)
-                part_z(i, ch, i, f + 2).start()
-
-            @pl.when(down < z)
-            def _():
-                combine(down, ch, has_right)
-                part_z(down, ch, down_slot, f - 2).start()
+        @pl.loop(0, CHUNKS + 1)
+        def _(turn):
+            up_ch, down_ch = turn - up_late, turn - 1 + up_late
+
+            @pl.when((i > z) & (up_ch >= 0) & (up_ch < CHUNKS))
+            def _():
+                send_sum(i, up_ch, has_left, i, f + 2)
+
+            @pl.when((down < z) & (down_ch >= 0) & (down_ch < CHUNKS))
+            def _():
+                send_sum(down, down_ch, has_right, down_slot, f - 2)
 
     lax.fori_loop(1, nz + 1, main_step, 0)
     reduce_step(nz - 1)
@@ -556,6 +572,7 @@
         ((NP, R, LANES), f32),
         ((NP, R, LANES), f32),
         ((R, LANES), f32),
+        ((NP, R, LANES), f32),
     ]
     size = sum(functools.reduce(lambda a, b: a * b, shape) * jnp.dtype(kind).itemsize for shape, kind in arrays)
     return arrays, size

time: 247 us -> 218 us (0.88)
  Pallas kernels: 243 us -> 213 us
    pallas_call x1, Pallas kernels: 243 us -> 213 us  [fused_shards(): pl.pallas_call(functools.partial(fused_kernel, nz, nctx), out_shape=jax.S...]
where the time goes in v4:
time: 218 us; the launch traced here: 216 us
  Pallas kernels  213 us (98%)
  local copies, waits for them, and re-layouts  2.29 us (1%)
    pallas_call x1, Pallas kernels, fused_shards(): pl.pallas_call(functools.partial(fused_kernel, nz, nctx), out_shape=jax.S...  213 us

profile of v4, /device:TPU:0, one launch (start us, length us, event | category | flops | bytes accessed | tf_op | source)
XLA Modules:
  0.0 215.6 jit_solution(11026591374893186574)
XLA Ops:
  0.0 213.4 %shard_map.82 = bf16[128,4096]{1,0:T(8,128)(2,1)} custom-call(bf16[128,4096]{1,0:T(8,128)(2,1)} %bitcast.7, f32[1,4096]{1,0:T(1,128)} %bitcast.8, bf16[3,4096,512]{2,1,0:T(8,128)(2,1)} %bitcast.5, f32[3,3,512]{2,1,0:T(4,128)} %taps_in.1, f32[16,512]{1,0:T(8,128)} %decay_in.1, f32[16,512]{1,0:T(8,128)} %residues_in.1, f32[1,512]{1,0:T(1,128)} %bitcast.9, ...), custom_call_target="tpu_custom_call" | custom-call | tf_op jit(solution)/shard_map/pallas_call | solution.py:589
  213.4 2.3 %copy.10 = bf16[1,128,4096]{2,1,0:T(8,128)(2,1)} copy(bf16[1,128,4096]{2,1,0:T(8,128)(2,1)} %bitcast.6) | data formatting | bytes 2097152

commit v5 on v4

--- a/solution.py
+++ b/solution.py
@@ -97,7 +97,9 @@
     return (values[0] + summed).astype(jnp.bfloat16)[None]
 
 
-CHUNKS = 4
+CHUNKS = 8
+ONCE = 2
+LAG = 2
 COLUMNS = 256
 STRIP = 16
 UNROLL = 4
@@ -210,18 +212,19 @@
             skip[row : row + 1, :] = skip_in[0:1, lanes]
     factor[...] = jnp.exp(-decay[...])
 
-    ag(partner, 0, X).wait_recv()
-
-    @pl.when(has_right)
-    def _():
-        ag(partner, 0, UP).start()
-
-    @pl.when(has_left)
-    def _():
-        ag(partner, 0, DOWN).start()
+    for ch in range(ONCE):
+        ag(partner, ch, X).wait_recv()
+
+        @pl.when(has_right)
+        def _():
+            ag(partner, ch, UP).start()
+
+        @pl.when(has_left)
+        def _():
+            ag(partner, ch, DOWN).start()
 
     def compute(p):
-        @pl.loop(1, CHUNKS)
+        @pl.loop(ONCE, CHUNKS)
         def _(ch):
             ag(p * 2 + 1 - x, ch, X).wait_recv()
 
@@ -273,7 +276,7 @@
             state = tuple(factor[n] * state[n] + product for n in range(NP))
         state = lax.fori_loop(1, T // UNROLL, first_pass, state)
         for n in range(NP):
-            st_tx[p, n] = state[n]
+            inc[n] = state[n]
 
         @pl.when(c > 0)
         def _():
@@ -286,7 +289,9 @@
 
         early = [filter_row(t * R) for t in range(2)]
         for n in range(NP):
-            st_tx[p, n] += (factor[n] * early[0] + early[1]) * jnp.exp(decay[n] * (-float(T - 2)))
+            inc[n] += (factor[n] * early[0] + early[1]) * jnp.exp(decay[n] * (-float(T - 2)))
+
+        st_tx[p] = inc[...].reshape(NP * R, LANES).astype(jnp.bfloat16)
 
         def state_copy(d):
             return remote(
@@ -303,7 +308,9 @@
             @pl.when(c >= d)
             def _():
                 state_copy(d).wait_recv()
-                inc[...] += jnp.exp(decay[...] * (-float(T * (d - 1)))) * st_rx[p, d - 1]
+                inc[...] += jnp.exp(decay[...] * (-float(T * (d - 1)))) * (
+                    st_rx[p, d - 1].astype(jnp.float32).reshape(NP, R, LANES)
+                )
 
         def second_pass(block, state):
             decays = [factor[n] for n in range(NP)]
@@ -331,7 +338,7 @@
                 gated_rows[...], wo_v[:, where], preferred_element_type=jnp.float32
             ).astype(jnp.bfloat16)
 
-        @pl.loop(1, CHUNKS)
+        @pl.loop(ONCE, CHUNKS)
         def _(ch):
             part_x(p, ch).start()
 
@@ -358,15 +365,17 @@
                     ag(block, ch, way).start()
 
             for column in range(2):
-                @pl.when(z - h >= 0)
-                def _():
-                    relay((z - h) * 2 + column, 0, UP)
-
-                @pl.when(z + h < nz)
-                def _():
-                    relay((z + h) * 2 + column, 0, DOWN)
-
-            @pl.loop(1, CHUNKS)
+                @pl.loop(0, ONCE)
+                def _(ch):
+                    @pl.when(z - h >= 0)
+                    def _():
+                        relay((z - h) * 2 + column, ch, UP)
+
+                    @pl.when(z + h < nz)
+                    def _():
+                        relay((z + h) * 2 + column, ch, DOWN)
+
+            @pl.loop(ONCE, CHUNKS)
             def _(ch):
                 @pl.when(z - h >= 0)
                 def _():
@@ -421,11 +430,11 @@
                 total = load(part, start, k) + load(rxx, other, k)
                 part[rows(start + k * STRIP, STRIP), :] = total.astype(jnp.bfloat16)
 
-    def other_z(p, slot, target):
+    def other_z(p, ch, slot, target):
         return remote(
-            part.at[rows((p * 2 + 1 - x) * T, TC), :],
-            rzo.at[rows(slot * TC, TC), :],
-            o_send.at[p], o_recv.at[slot], {"fsdp": target},
+            part.at[rows((p * 2 + 1 - x) * T + ch * TC, TC), :],
+            rzo.at[rows((slot * ONCE + ch) * TC, TC), :],
+            o_send.at[p, ch], o_recv.at[slot, ch], {"fsdp": target},
         )
 
     def add_in(start, ref, begin):
@@ -434,27 +443,27 @@
             total = load(part, start, k) + load(ref, begin, k)
             part[rows(start + k * STRIP, STRIP), :] = total.astype(jnp.bfloat16)
 
-    def first_chunk(p, more, slot, target):
+    def first_chunk(p, ch, more, slot, target):
         @pl.when(more)
         def _():
-            part_z(p, 0, p, partner).wait_recv()
-            add_in((p * 2 + x) * T, rz, p * T)
-
-        part_z(p, 0, slot, target).start()
+            part_z(p, ch, p, partner).wait_recv()
+            add_in((p * 2 + x) * T + ch * TC, rz, p * T + ch * TC)
+
+        part_z(p, ch, slot, target).start()
 
         @pl.when(more)
         def _():
-            other_z(p, p, partner).wait_recv()
-            add_in((p * 2 + 1 - x) * T, rzo, p * TC)
-
-        other_z(p, slot, target).start()
+            other_z(p, ch, p, partner).wait_recv()
+            add_in((p * 2 + 1 - x) * T + ch * TC, rzo, (p * ONCE + ch) * TC)
+
+        other_z(p, ch, slot, target).start()
 
     def send_sum(p, ch, more, slot, target):
-        @pl.when(ch == 0)
-        def _():
-            first_chunk(p, more, slot, target)
-
-        @pl.when(ch > 0)
+        @pl.when(ch < ONCE)
+        def _():
+            first_chunk(p, ch, more, slot, target)
+
+        @pl.when(ch >= ONCE)
         def _():
             combine(p, ch, more)
             part_z(p, ch, slot, target).start()
@@ -465,9 +474,9 @@
         down = nz - 1 - i
         down_slot = jnp.where(down == z - 1, nz, down)
 
-        @pl.loop(0, CHUNKS + 1)
+        @pl.loop(0, CHUNKS + LAG)
         def _(turn):
-            up_ch, down_ch = turn - up_late, turn - 1 + up_late
+            up_ch, down_ch = turn - LAG * up_late, turn - LAG * (1 - up_late)
 
             @pl.when((i > z) & (up_ch >= 0) & (up_ch < CHUNKS))
             def _():
@@ -480,17 +489,18 @@
     lax.fori_loop(1, nz + 1, main_step, 0)
     reduce_step(nz - 1)
 
-    for more, slot in ((has_left, z), (has_right, nz)):
-        @pl.when(more)
-        def _():
-            other_z(z, slot, partner).wait_recv()
-            add_in(partner * T, rzo, slot * TC)
-
-    part_x(z, 0).start()
+    for ch in range(ONCE):
+        for more, slot in ((has_left, z), (has_right, nz)):
+            @pl.when(more)
+            def _():
+                other_z(z, ch, slot, partner).wait_recv()
+                add_in(partner * T + ch * TC, rzo, (slot * ONCE + ch) * TC)
+
+        part_x(z, ch).start()
 
     @pl.loop(0, CHUNKS)
     def _(turn):
-        ch = lax.rem(turn + 1, CHUNKS)
+        ch = lax.rem(turn + ONCE, CHUNKS)
         start = ch * TC
         part_x(z, ch).wait_recv()
 
@@ -517,7 +527,7 @@
     def _(p):
         @pl.loop(0, CHUNKS)
         def _(ch):
-            @pl.when((ch > 0) | (p == z))
+            @pl.when((ch >= ONCE) | (p == z))
             def _():
                 ag(p * 2 + x, ch, X).wait_send()
                 part_x(p, ch).wait_send()
@@ -534,17 +544,19 @@
             def _():
                 part_z(p, ch, p, partner).wait_send()
 
-        @pl.when((p <= z) & has_right)
-        def _():
-            ag(p * 2 + 1 - x, 0, UP).wait_send()
-
-        @pl.when((p >= z) & has_left)
-        def _():
-            ag(p * 2 + 1 - x, 0, DOWN).wait_send()
-
-        @pl.when(p != z)
-        def _():
-            other_z(p, p, partner).wait_send()
+        @pl.loop(0, ONCE)
+        def _(ch):
+            @pl.when((p <= z) & has_right)
+            def _():
+                ag(p * 2 + 1 - x, ch, UP).wait_send()
+
+            @pl.when((p >= z) & has_left)
+            def _():
+                ag(p * 2 + 1 - x, ch, DOWN).wait_send()
+
+            @pl.when(p != z)
+            def _():
+                other_z(p, ch, p, partner).wait_send()
 
 
 def scratch_of(nz, nctx, T, D, C, NP):
@@ -563,11 +575,11 @@
         ((T * R, LANES), f32),
         ((2 * T, C), bf16),
         ((nz, 3, 2 * R, LANES), f32),
-        ((nz, NP, R, LANES), f32),
-        ((nz, nctx - 1, NP, R, LANES), f32),
+        ((nz, NP * R, LANES), bf16),
+        ((nz, nctx - 1, NP * R, LANES), bf16),
         ((NP, R, LANES), f32),
         ((T // CHUNKS, D), f32),
-        (((nz + 1) * T // CHUNKS, D), bf16),
+        (((nz + 1) * ONCE * T // CHUNKS, D), bf16),
         ((3, 3, R, LANES), f32),
         ((NP, R, LANES), f32),
         ((NP, R, LANES), f32),
@@ -600,8 +612,8 @@
             dma((nz, CHUNKS)),
             dma((nz, CHUNKS)),
             dma((nz + 1, CHUNKS)),
-            dma((nz,)),
-            dma((nz + 1,)),
+            dma((nz, ONCE)),
+            dma((nz + 1, ONCE)),
             dma((nz,)),
             dma((nz,)),
             dma((nz, nctx - 1)),

time: 218 us -> 217 us (level)
  no operation moved by 1% of the time
where the time goes in v5:
time: 217 us; the launch traced here: 216 us
  Pallas kernels  213 us (98%)
  local copies, waits for them, and re-layouts  2.29 us (1%)
    pallas_call x1, Pallas kernels, fused_shards(): pl.pallas_call(functools.partial(fused_kernel, nz, nctx), out_shape=jax.S...  213 us

profile of v5, /device:TPU:0, one launch (start us, length us, event | category | flops | bytes accessed | tf_op | source)
XLA Modules:
  0.0 215.6 jit_solution(15674138497393585598)
XLA Ops:
  0.0 213.3 %shard_map.82 = bf16[128,4096]{1,0:T(8,128)(2,1)} custom-call(bf16[128,4096]{1,0:T(8,128)(2,1)} %bitcast.7, f32[1,4096]{1,0:T(1,128)} %bitcast.8, bf16[3,4096,512]{2,1,0:T(8,128)(2,1)} %bitcast.5, f32[3,3,512]{2,1,0:T(4,128)} %taps_in.1, f32[16,512]{1,0:T(8,128)} %decay_in.1, f32[16,512]{1,0:T(8,128)} %residues_in.1, f32[1,512]{1,0:T(1,128)} %bitcast.9, ...), custom_call_target="tpu_custom_call" | custom-call | tf_op jit(solution)/shard_map/pallas_call | solution.py:601
  213.3 2.3 %copy.10 = bf16[1,128,4096]{2,1,0:T(8,128)(2,1)} copy(bf16[1,128,4096]{2,1,0:T(8,128)(2,1)} %bitcast.6) | data formatting | bytes 2097152

commit v6 on v5

--- a/solution.py
+++ b/solution.py
@@ -223,7 +223,7 @@
         def _():
             ag(partner, ch, DOWN).start()
 
-    def compute(p):
+    def compute(p, meanwhile):
         @pl.loop(ONCE, CHUNKS)
         def _(ch):
             ag(p * 2 + 1 - x, ch, X).wait_recv()
@@ -303,6 +303,7 @@
             def _():
                 state_copy(d).start()
 
+        meanwhile()
         inc[...] = jnp.zeros(inc.shape, jnp.float32)
         for d in range(1, nctx):
             @pl.when(c >= d)
@@ -338,9 +339,11 @@
                 gated_rows[...], wo_v[:, where], preferred_element_type=jnp.float32
             ).astype(jnp.bfloat16)
 
-        @pl.loop(ONCE, CHUNKS)
-        def _(ch):
-            part_x(p, ch).start()
+        @pl.when(p != z)
+        def _():
+            @pl.loop(ONCE, CHUNKS)
+            def _(ch):
+                part_x(p, ch).start()
 
         @pl.when(c + 1 < nctx)
         def _():
@@ -389,12 +392,17 @@
                     relay(block, ch, DOWN)
                     ag(block, ch, X).start()
 
+        def meanwhile():
+            @pl.when(h > 2)
+            def _():
+                reduce_step(h - 2, jnp.logical_not(has_left), jnp.logical_not(has_right))
+
         def side_step(side, carry):
             p = z + (h - 1) * (2 * side - 1)
 
             @pl.when((p >= 0) & (p < nz) & ((h > 1) | (side == 0)))
             def _():
-                compute(p)
+                compute(p, meanwhile)
 
             return carry
 
@@ -402,7 +410,7 @@
 
         @pl.when(h > 2)
         def _():
-            reduce_step(h - 2)
+            reduce_step(h - 2, has_left, has_right)
 
         return carry
 
@@ -470,7 +478,7 @@
 
     up_late = (2 * z >= nz).astype(jnp.int32)
 
-    def reduce_step(i):
+    def reduce_step(i, ups, downs):
         down = nz - 1 - i
         down_slot = jnp.where(down == z - 1, nz, down)
 
@@ -478,16 +486,21 @@
         def _(turn):
             up_ch, down_ch = turn - LAG * up_late, turn - LAG * (1 - up_late)
 
-            @pl.when((i > z) & (up_ch >= 0) & (up_ch < CHUNKS))
+            @pl.when(ups & (i > z) & (up_ch >= 0) & (up_ch < CHUNKS))
             def _():
                 send_sum(i, up_ch, has_left, i, f + 2)
 
-            @pl.when((down < z) & (down_ch >= 0) & (down_ch < CHUNKS))
+            @pl.when(downs & (down < z) & (down_ch >= 0) & (down_ch < CHUNKS))
             def _():
                 send_sum(down, down_ch, has_right, down_slot, f - 2)
 
     lax.fori_loop(1, nz + 1, main_step, 0)
-    reduce_step(nz - 1)
+
+    @pl.loop(ONCE, CHUNKS)
+    def _(ch):
+        part_x(z, ch).start()
+
+    reduce_step(nz - 1, True, True)
 
     for ch in range(ONCE):
         for more, slot in ((has_left, z), (has_right, nz)):

time: 217 us -> 206 us (0.949)
  Pallas kernels: 213 us -> 204 us
    pallas_call x1, Pallas kernels: 213 us -> 204 us  [fused_shards(): pl.pallas_call(functools.partial(fused_kernel, nz, nctx), out_shape=jax.S...]
where the time goes in v6:
time: 206 us
  Pallas kernels  204 us (99%)
  local copies, waits for them, and re-layouts  2.29 us (1%)
    pallas_call x1, Pallas kernels, fused_shards(): pl.pallas_call(functools.partial(fused_kernel, nz, nctx), out_shape=jax.S...  204 us

profile of v6, /device:TPU:0, one launch (start us, length us, event | category | flops | bytes accessed | tf_op | source)
XLA Modules:
  0.0 205.9 jit_solution(10086873340256796852)
XLA Ops:
  0.0 203.6 %shard_map.82 = bf16[128,4096]{1,0:T(8,128)(2,1)} custom-call(bf16[128,4096]{1,0:T(8,128)(2,1)} %bitcast.7, f32[1,4096]{1,0:T(1,128)} %bitcast.8, bf16[3,4096,512]{2,1,0:T(8,128)(2,1)} %bitcast.5, f32[3,3,512]{2,1,0:T(4,128)} %taps_in.1, f32[16,512]{1,0:T(8,128)} %decay_in.1, f32[16,512]{1,0:T(8,128)} %residues_in.1, f32[1,512]{1,0:T(1,128)} %bitcast.9, ...), custom_call_target="tpu_custom_call" | custom-call | tf_op jit(solution)/shard_map/pallas_call | solution.py:614
  203.6 2.3 %copy.10 = bf16[1,128,4096]{2,1,0:T(8,128)(2,1)} copy(bf16[1,128,4096]{2,1,0:T(8,128)(2,1)} %bitcast.6) | data formatting | bytes 2097152
